TPU v7x, 128 devices: a whole 4x4x4 slice. The times are simulated.
128 devices in a mesh: grp: 4 (over y_lo, core), dev: 32 (over x, z, y_hi).
Axes of the slice: x: 4, y: 4 (y_hi: 2, y_lo: 2; y = y_hi * 2 + y_lo), z: 4, core: 2. Of those that a mesh axis runs over, the one named last changes fastest.
Arguments:
- tokens: bfloat16 [16384, 2048], P(('grp', 'dev')), may hold values from -6 to 6
- cotangent: bfloat16 [16384, 2048], P(('grp', 'dev')), may hold values from -1.5 to 1.5
- route_weight: float32 [16384, 2], P(('grp', 'dev')), may hold values from 0.1 to 1
- slot_expert: int32 [128], replicated, may hold values from 0 to 15, as said below
- targets: int32 [16384, 2], P(('grp', 'dev')), may hold values from 0 to 127, as said below
- proj_in: float32 [16, 2048, 2048], P('grp', 'dev'), may hold values from -0.125 to 0.125
- first_in: float32 [16, 2048, 2048], P('grp', 'dev'), may hold values from -6 to 6
- second_in: float32 [16, 2048, 2048], P('grp', 'dev'), may hold values from 0.01 to 1
- proj_out: float32 [16, 1024, 2048], P('grp', 'dev'), may hold values from -0.1875 to 0.1875
- first_out: float32 [16, 1024, 2048], P('grp', 'dev'), may hold values from -6 to 6
- second_out: float32 [16, 1024, 2048], P('grp', 'dev'), may hold values from 0.01 to 1
Outputs:
- mixed: bfloat16 [16384, 2048], P(('grp', 'dev'))
- token_grad: bfloat16 [16384, 2048], P(('grp', 'dev'))
- mix_grad: float32 [16384, 2], P(('grp', 'dev'))
- trained_in: float32 [16, 2048, 2048], P('grp', 'dev')
- mean_in: float32 [16, 2048, 2048], P('grp', 'dev')
- square_in: float32 [16, 2048, 2048], P('grp', 'dev')
- trained_out: float32 [16, 1024, 2048], P('grp', 'dev')
- mean_out: float32 [16, 1024, 2048], P('grp', 'dev')
- square_out: float32 [16, 1024, 2048], P('grp', 'dev')
Inputs may be any that keep to these rules, and one draw needn't show every extreme that they name: `slot_expert`: entry s is the expert held by slot s, the device s in grp+dev order; each of the 16 experts is held by at least one slot. `targets`: entry [t, k] is the slot that serves the k-th expert of token t; the two slots of a token hold different experts.
All inputs are finite; a program needn't handle non-finite values.
Results may differ from a plain program's by a relative error of at most 0.015.
The roundings to bfloat16 on the way count: a program that leaves them out, or rounds other values in their place, can miss the bound.
Values may be sent and summed in bfloat16 or wider, within the bound.
No kernel may reach another device: no remote copies, remote signals or barrier semaphores. Data moves between devices by JAX's collectives and lax.ppermute only.
A program may use at most 128 MiB of HBM per device.

v0:
```python
import jax
import jax.numpy as jnp
from jax import lax
from jax.sharding import PartitionSpec as P

D = 2048
FF = 1024
E = 16
beta_first = 0.9
beta_second = 0.95
learn_rate = 0.01
decay_rate = 0.1
adam_eps = 1e-08
bias_first = 1.0 - 0.9**10
bias_second = 1.0 - 0.95**10


def silu_parts(values):
    logistic = jax.nn.sigmoid(values)
    return (values * logistic, logistic * (1.0 + values * (1.0 - logistic)))


def slot_pass(rows_x, rows_dy, weight_up, weight_down):
    gate_up = jnp.dot(rows_x, weight_up, preferred_element_type=jnp.float32)
    gating = gate_up[:, :FF]
    upward = gate_up[:, FF:]
    active, derivative = silu_parts(gating)
    hidden = (active * upward).astype(jnp.bfloat16)
    result = jnp.dot(hidden, weight_down, preferred_element_type=jnp.float32).astype(jnp.bfloat16)
    dhidden = lax.dot_general(
        rows_dy, weight_down, (((1,), (1,)), ((), ())), preferred_element_type=jnp.float32
    )
    grad_gateup = jnp.concatenate([dhidden * upward * derivative, dhidden * active], axis=1).astype(
        jnp.bfloat16
    )
    rows_dx = lax.dot_general(
        grad_gateup, weight_up, (((1,), (1,)), ((), ())), preferred_element_type=jnp.float32
    ).astype(jnp.bfloat16)
    grad_up = lax.dot_general(
        rows_x, grad_gateup, (((0,), (0,)), ((), ())), preferred_element_type=jnp.float32
    ).astype(jnp.bfloat16)
    grad_down = lax.dot_general(
        hidden, rows_dy, (((0,), (0,)), ((), ())), preferred_element_type=jnp.float32
    ).astype(jnp.bfloat16)
    return (result, rows_dx, grad_up, grad_down)


def adam_step(weight, moment, square, gradient):
    new_moment = beta_first * moment + (1.0 - beta_first) * gradient
    new_square = beta_second * square + (1.0 - beta_second) * gradient * gradient
    update = (
        new_moment / bias_first / (jnp.sqrt(new_square / bias_second) + adam_eps)
        + decay_rate * weight
    )
    return (weight - learn_rate * update, new_moment, new_square)


def to_slots(payload_x, payload_dy):
    moved_x, moved_dy = (
        lax.all_to_all(payload_x, ("grp", "dev"), split_axis=0, concat_axis=0, tiled=True),
        lax.all_to_all(payload_dy, ("grp", "dev"), split_axis=0, concat_axis=0, tiled=True),
    )
    return (moved_x, moved_dy)


def to_sources(payload_out, payload_dx):
    moved_out, moved_dx = (
        lax.all_to_all(payload_out, ("grp", "dev"), split_axis=0, concat_axis=0, tiled=True),
        lax.all_to_all(payload_dx, ("grp", "dev"), split_axis=0, concat_axis=0, tiled=True),
    )
    return (moved_out, moved_dx)


def on_device(
    tokens,
    cotangent,
    route_weight,
    slot_expert,
    targets,
    proj_in,
    first_in,
    second_in,
    proj_out,
    first_out,
    second_out,
):
    groups = lax.axis_size("grp")
    members = lax.axis_size("dev")
    slot_count = groups * members
    tok_count = tokens.shape[0]
    assigns = 2 * tok_count
    capacity = 3 * tok_count // slot_count
    buffer_rows = slot_count * capacity
    flat_target = targets.reshape(-1)
    onehot = (flat_target[:, None] == jnp.arange(slot_count, dtype=jnp.int32)[None, :]).astype(
        jnp.int32
    )
    earlier = jnp.cumsum(onehot, axis=0) - onehot
    position = jnp.sum(earlier * onehot, axis=1)
    within = position < capacity
    dest_row = jnp.where(within, flat_target * capacity + position, buffer_rows)
    matched = dest_row[:, None] == jnp.arange(buffer_rows, dtype=jnp.int32)[None, :]
    filled = jnp.any(matched, axis=0)
    source_id = jnp.sum(
        jnp.where(matched, jnp.arange(assigns, dtype=jnp.int32)[:, None], 0), axis=0
    )
    scaled = (
        route_weight.reshape(-1)[:, None] * jnp.repeat(cotangent, 2, axis=0).astype(jnp.float32)
    ).astype(jnp.bfloat16)
    send_x = jnp.where(filled[:, None], tokens[source_id // 2], jnp.zeros((), jnp.bfloat16))
    send_dy = jnp.where(filled[:, None], scaled[source_id], jnp.zeros((), jnp.bfloat16))
    slot_x, slot_dy = to_slots(
        send_x.reshape(slot_count, capacity, D), send_dy.reshape(slot_count, capacity, D)
    )
    slot_x = slot_x.reshape(buffer_rows, D)
    slot_dy = slot_dy.reshape(buffer_rows, D)
    my_group = lax.axis_index("grp")
    group_expert = lax.dynamic_slice_in_dim(slot_expert, my_group * members, members)
    low_in = proj_in.astype(jnp.bfloat16)
    low_out = proj_out.astype(jnp.bfloat16)
    all_up, all_down = (
        lax.all_gather(low_in, "grp", axis=0, tiled=True),
        lax.all_gather(low_out, "grp", axis=0, tiled=True),
    )
    send_up = jnp.take(all_up, group_expert, axis=0)
    send_down = jnp.take(all_down, group_expert, axis=0)
    got_up, got_down = (
        lax.all_to_all(send_up, "dev", split_axis=0, concat_axis=0, tiled=True),
        lax.all_to_all(send_down, "dev", split_axis=0, concat_axis=0, tiled=True),
    )
    slot_up = got_up.reshape(D, 2 * FF)
    slot_down = got_down.reshape(FF, D)
    result, rows_dx, grad_up, grad_down = slot_pass(slot_x, slot_dy, slot_up, slot_down)
    back_out, back_dx = to_sources(
        result.reshape(slot_count, capacity, D), rows_dx.reshape(slot_count, capacity, D)
    )
    flat_out = back_out.reshape(buffer_rows, D)
    flat_dx = back_dx.reshape(buffer_rows, D)
    pick_row = jnp.where(within, flat_target * capacity + position, 0)
    assigned_out = jnp.where(
        within[:, None], flat_out[pick_row], jnp.zeros((), jnp.bfloat16)
    ).reshape(tok_count, 2, D)
    assigned_dx = jnp.where(
        within[:, None], flat_dx[pick_row], jnp.zeros((), jnp.bfloat16)
    ).reshape(tok_count, 2, D)
    out_float = assigned_out.astype(jnp.float32)
    mixed = (
        route_weight[:, 0:1] * out_float[:, 0] + route_weight[:, 1:2] * out_float[:, 1]
    ).astype(jnp.bfloat16)
    token_grad = (
        assigned_dx[:, 0].astype(jnp.float32) + assigned_dx[:, 1].astype(jnp.float32)
    ).astype(jnp.bfloat16)
    mix_grad = jnp.sum(cotangent.astype(jnp.float32)[:, None, :] * out_float, axis=2)
    rows_up, rows_down = (
        lax.all_to_all(
            grad_up.reshape(members, D // members, 2 * FF),
            "dev",
            split_axis=0,
            concat_axis=0,
            tiled=True,
        ),
        lax.all_to_all(
            grad_down.reshape(members, FF // members, D),
            "dev",
            split_axis=0,
            concat_axis=0,
            tiled=True,
        ),
    )
    holder = (group_expert[None, :] == jnp.arange(E, dtype=jnp.int32)[:, None]).astype(jnp.bfloat16)
    part_up = jnp.einsum("ed,drc->erc", holder, rows_up, preferred_element_type=jnp.float32)
    part_down = jnp.einsum("ed,drc->erc", holder, rows_down, preferred_element_type=jnp.float32)
    sum_up, sum_down = (
        lax.psum_scatter(
            part_up.astype(jnp.bfloat16), "grp", scatter_dimension=0, tiled=True
        ).astype(jnp.float32),
        lax.psum_scatter(
            part_down.astype(jnp.bfloat16), "grp", scatter_dimension=0, tiled=True
        ).astype(jnp.float32),
    )
    trained_in, mean_in, square_in = adam_step(proj_in, first_in, second_in, sum_up)
    trained_out, mean_out, square_out = adam_step(proj_out, first_out, second_out, sum_down)
    return (
        mixed,
        token_grad,
        mix_grad,
        trained_in,
        mean_in,
        square_in,
        trained_out,
        mean_out,
        square_out,
    )


def solution(mesh):
    in_specs = (
        P(("grp", "dev"), None),
        P(("grp", "dev"), None),
        P(("grp", "dev"), None),
        P(),
        P(("grp", "dev"), None),
        P("grp", "dev", None),
        P("grp", "dev", None),
        P("grp", "dev", None),
        P("grp", "dev", None),
        P("grp", "dev", None),
        P("grp", "dev", None),
    )
    out_specs = (
        P(("grp", "dev"), None),
        P(("grp", "dev"), None),
        P(("grp", "dev"), None),
        P("grp", "dev", None),
        P("grp", "dev", None),
        P("grp", "dev", None),
        P("grp", "dev", None),
        P("grp", "dev", None),
        P("grp", "dev", None),
    )
    return jax.shard_map(
        on_device, mesh=mesh, in_specs=in_specs, out_specs=out_specs, check_vma=False
    )
```

profile of v0, /device:TPU:1, one launch (start us, length us, event | category | flops | bytes accessed | tf_op | source)
XLA Modules:
  0.0 679.6 jit_solution(7755972250965304729)
XLA Ops:
  7.3 2.8 convert_element_type.80
  11.6 2.4 convert_element_type.87
  16.8 3.1 gather_fusion.4
  19.9 4.0 gather.35
  24.3 3.1 gather_fusion
  27.5 5.2 gather.29
  32.6 4.3 broadcast_select_fusion.2
  36.9 44.3 %all_to_all.40 = bf16[128,3,2048]{2,1,0:T(4,128)(2,1)S(1)} all-to-all(bf16[128,3,2048]{2,1,0:T(4,128)(2,1)S(1)} %get-tuple-element.59), channel_id=1, replica_groups=mesh['grp'=4,'dev'=32] {'grp','dev'}, dimensions={0} | all-to-all | bytes 3145728 | tf_op jit(solution)/shard_map/all_to_all | solution.py:60
  81.3 7.1 %all-to-all-start.4 = ((bf16[128,3,2048]{2,1,0:T(4,128)(2,1)}), bf16[128,3,2048]{2,1,0:T(4,128)(2,1)}, u32[]{:S(2)}, u32[]{:S(2)}) async-start(bf16[128,3,2048]{2,1,0:T(4,128)(2,1)} %get-tuple-element.58), calls=%async_computation.4 | async-start | bytes 4194304 | tf_op jit(solution)/shard_map/all_to_all | solution.py:61
  88.5 7.2 %gather_fusion.1 = bf16[32,64,2048]{2,1,0:T(8,128)(2,1)} fusion(bf16[16,64,2048]{2,1,0:T(8,128)(2,1)} %all-gather.3.cloned.1.call-done, s32[1024]{0:T(1024)S(1)} %pad_clamp_fusion.2), kind=kCustom, calls=%fused_computation.1 | custom fusion | bytes 16777344 | tf_op jit(solution)/shard_map/jit(_take)/gather | solution.py:125
  95.7 7.5 %broadcast_select_fusion = bf16[32,64,2048]{2,1,0:T(8,128)(2,1)} fusion(bf16[32,64,2048]{2,1,0:T(8,128)(2,1)} %gather_fusion.1, pred[32]{0:T(512)(128)(4,1)S(1)} %get-tuple-element.53), kind=kLoop, calls=%fused_computation.8 | loop fusion | flops 4194304 | bytes 16777248 | tf_op jit(solution)/shard_map/jit(_take)/select_n | solution.py:125
  103.2 15.1 %all-to-all-done.4 = bf16[128,3,2048]{2,1,0:T(4,128)(2,1)} async-done(((bf16[128,3,2048]{2,1,0:T(4,128)(2,1)}), bf16[128,3,2048]{2,1,0:T(4,128)(2,1)}, u32[]{:S(2)}, u32[]{:S(2)}) %all-to-all-start.4) | async-done | bytes 1572896 | tf_op jit(solution)/shard_map/all_to_all | solution.py:61
  118.2 5.0 all-to-all-start.1
  125.3 106.8 %all-gather.5.cloned.1.call-done = bf16[16,32,2048]{2,1,0:T(8,128)(2,1)} async-done(((bf16[4,32,2048]{2,1,0:T(8,128)(2,1)}), bf16[16,32,2048]{2,1,0:T(8,128)(2,1)}) %all-gather.5.cloned.1.call-update) | async-done | bytes 2097168 | tf_op jit(solution)/shard_map/all_gather | solution.py:123
  232.2 4.4 gather_fusion.2
  236.5 4.6 broadcast_select_fusion.1
  241.2 7.3 %all-to-all-done.1 = bf16[32,64,2048]{2,1,0:T(8,128)(2,1)} async-done(((bf16[32,64,2048]{2,1,0:T(8,128)(2,1)}), bf16[32,64,2048]{2,1,0:T(8,128)(2,1)}, u32[]{:S(2)}, u32[]{:S(2)}) %all-to-all-start.1) | async-done | bytes 8388640 | tf_op jit(solution)/shard_map/all_to_all | solution.py:128
  248.4 13.3 %all-to-all-start.2 = ((bf16[32,32,2048]{2,1,0:T(8,128)(2,1)}), bf16[32,32,2048]{2,1,0:T(8,128)(2,1)}, u32[]{:S(2)}, u32[]{:S(2)}) async-start(bf16[32,32,2048]{2,1,0:T(8,128)(2,1)} %broadcast_select_fusion.1), calls=%async_computation.2 | async-start | bytes 8388608 | tf_op jit(solution)/shard_map/all_to_all | solution.py:129
  261.7 2.5 reshape.237
  264.2 5.2 reshape.242
  269.3 8.5 %fusion.40 = f32[384,2048]{1,0:T(8,128)} fusion(bf16[384,2048]{1,0:T(8,128)(2,1)S(1)} %copy-done.5, bf16[2048,2048]{1,0:T(8,128)(2,1)} %bitcast.4), kind=kOutput, calls=%fused_computation.89 | convolution fusion | flops 3221225472 | bytes 13107200 | tf_op jit(solution)/shard_map/dot_general | solution.py:24
  277.8 38.0 %all-to-all-done.2 = bf16[32,32,2048]{2,1,0:T(8,128)(2,1)} async-done(((bf16[32,32,2048]{2,1,0:T(8,128)(2,1)}), bf16[32,32,2048]{2,1,0:T(8,128)(2,1)}, u32[]{:S(2)}, u32[]{:S(2)}) %all-to-all-start.2) | async-done | bytes 4194336 | tf_op jit(solution)/shard_map/all_to_all | solution.py:129
  315.9 7.2 %multiply_convert_fusion.2 = (bf16[384,1024]{1,0:T(8,128)(2,1)}, bf16[384,1024]{1,0:T(8,128)(2,1)}, bf16[384,1024]{1,0:T(8,128)(2,1)S(1)}) fusion(f32[384,2048]{1,0:T(8,128)} %fusion.40, bf16[384,2048]{1,0:T(8,128)(2,1)} %reshape.242, bf16[1024,2048]{1,0:T(8,128)(2,1)} %bitcast.5), kind=kOutput, calls=%fused_computation.30 | convolution fusion | flops 1616510976 | bytes 11272192 | tf_op jit(solution)/shard_map/dot_general | solution.py:30
  323.0 4.4 convolution_convert_fusion.1
  327.4 8.8 %all-to-all-start.7 = ((bf16[32,32,2048]{2,1,0:T(8,128)(2,1)}), bf16[32,32,2048]{2,1,0:T(8,128)(2,1)}, u32[]{:S(2)}, u32[]{:S(2)}) async-start(bf16[32,32,2048]{2,1,0:T(8,128)(2,1)} %bitcast.54), calls=%async_computation.8 | async-start | bytes 8388608 | tf_op jit(solution)/shard_map/all_to_all | solution.py:162
  336.2 8.1 %convolution_convert_fusion = bf16[2048,2048]{1,0:T(8,128)(2,1)} fusion(bf16[384,2048]{1,0:T(8,128)(2,1)S(1)} %copy-done.5, bf16[384,1024]{1,0:T(8,128)(2,1)} %get-tuple-element.56, bf16[384,1024]{1,0:T(8,128)(2,1)} %get-tuple-element.55), kind=kOutput, calls=%fused_computation.9 | convolution fusion | flops 3228565504 | bytes 11534336 | tf_op jit(solution)/shard_map/dot_general | solution.py:39
  344.3 45.0 %all-to-all-done.7 = bf16[32,32,2048]{2,1,0:T(8,128)(2,1)} async-done(((bf16[32,32,2048]{2,1,0:T(8,128)(2,1)}), bf16[32,32,2048]{2,1,0:T(8,128)(2,1)}, u32[]{:S(2)}, u32[]{:S(2)}) %all-to-all-start.7) | async-done | bytes 4194336 | tf_op jit(solution)/shard_map/all_to_all | solution.py:162
  389.3 9.3 %all-to-all-start.6 = ((bf16[32,64,2048]{2,1,0:T(8,128)(2,1)}), bf16[32,64,2048]{2,1,0:T(8,128)(2,1)}, u32[]{:S(2)}, u32[]{:S(2)}) async-start(bf16[32,64,2048]{2,1,0:T(8,128)(2,1)} %bitcast.53), calls=%async_computation.6 | async-start | bytes 16777216 | tf_op jit(solution)/shard_map/all_to_all | solution.py:155
  398.7 6.8 fusion.7
  405.5 2.5 copy.90
  408.0 8.8 %reduce-scatter.3.cloned.1.call-start = ((), (), s32[]{:S(2)}) async-start(), calls=%async_computation.12 | async-start | bytes 5242880 | tf_op jit(solution)/shard_map/reduce_scatter | solution.py:174
  416.8 103.2 %all-to-all-done.6 = bf16[32,64,2048]{2,1,0:T(8,128)(2,1)} async-done(((bf16[32,64,2048]{2,1,0:T(8,128)(2,1)}), bf16[32,64,2048]{2,1,0:T(8,128)(2,1)}, u32[]{:S(2)}, u32[]{:S(2)}) %all-to-all-start.6) | async-done | bytes 8388640 | tf_op jit(solution)/shard_map/all_to_all | solution.py:155
  520.0 12.5 %fusion.4 = bf16[16,64,2048]{2,0,1:T(8,128)(2,1)S(1)} fusion(bf16[32,64,2048]{2,1,0:T(8,128)(2,1)} %all-to-all-done.6, s32[32]{0:T(128)S(1)} %get-tuple-element.54), kind=kOutput, calls=%fused_computation.14 | convolution fusion | flops 136315392 | bytes 12583040 | tf_op jit(solution)/shard_map/ed,drc->erc/dot_general | solution.py:171
  532.5 4.3 copy.88
  536.8 7.5 %convolution_convert_fusion.2 = bf16[384,2048]{1,0:T(8,128)(2,1)S(1)} fusion(bf16[2048,2048]{1,0:T(8,128)(2,1)} %bitcast.4, bf16[384,1024]{1,0:T(8,128)(2,1)} %get-tuple-element.56, bf16[384,1024]{1,0:T(8,128)(2,1)} %get-tuple-element.55), kind=kOutput, calls=%fused_computation.17 | convolution fusion | flops 3225157632 | bytes 11534336 | tf_op jit(solution)/shard_map/dot_general | solution.py:36
  546.7 24.6 %all-to-all-start.5 = ((bf16[128,3,2048]{2,1,0:T(4,128)(2,1)}), bf16[128,3,2048]{2,1,0:T(4,128)(2,1)S(1)}, u32[]{:S(2)}, u32[]{:S(2)}) async-start(bf16[128,3,2048]{2,1,0:T(4,128)(2,1)} %reshape.243), calls=%async_computation.5 | async-start | bytes 4194304 | tf_op jit(solution)/shard_map/all_to_all | solution.py:69
  571.2 5.4 convolution_convert_fusion.3
  576.7 5.2 reshape.240
  581.8 22.4 %all-to-all-done.5 = bf16[128,3,2048]{2,1,0:T(4,128)(2,1)S(1)} async-done(((bf16[128,3,2048]{2,1,0:T(4,128)(2,1)}), bf16[128,3,2048]{2,1,0:T(4,128)(2,1)S(1)}, u32[]{:S(2)}, u32[]{:S(2)}) %all-to-all-start.5) | async-done | bytes 1572896 | tf_op jit(solution)/shard_map/all_to_all | solution.py:69
  605.5 7.5 %all-to-all-start.3 = ((bf16[128,3,2048]{2,1,0:T(4,128)(2,1)}), bf16[128,3,2048]{2,1,0:T(4,128)(2,1)}, u32[]{:S(2)}, u32[]{:S(2)}) async-start(bf16[128,3,2048]{2,1,0:T(4,128)(2,1)} %reshape.240), calls=%async_computation.3 | async-start | bytes 4194304 | tf_op jit(solution)/shard_map/all_to_all | solution.py:68
  613.6 3.9 reshape.244
  620.4 25.2 %all-to-all-done.3 = bf16[128,3,2048]{2,1,0:T(4,128)(2,1)} async-done(((bf16[128,3,2048]{2,1,0:T(4,128)(2,1)}), bf16[128,3,2048]{2,1,0:T(4,128)(2,1)}, u32[]{:S(2)}, u32[]{:S(2)}) %all-to-all-start.3) | async-done | bytes 1572896 | tf_op jit(solution)/shard_map/all_to_all | solution.py:68
  645.6 3.9 reshape.241
  649.5 2.3 gather_fusion.3
  651.8 2.7 gather.33
  656.9 2.9 copy_select_fusion
  661.7 4.4 multiply_subtract_fusion.1
  666.1 6.5 multiply_subtract_fusion
  (77 shorter events, 18.3 us)
Async XLA Ops:
  7.2 17.2 %copy-start = (bf16[128,2048]{1,0:T(8,128)(2,1)S(1)}, bf16[128,2048]{1,0:T(8,128)(2,1)}, u32[]{:S(2)}) copy-start(bf16[128,2048]{1,0:T(8,128)(2,1)} %param.11) | copy-start | bytes 1572868
  7.2 2.9 copy-start.8
  7.2 3.3 copy-start.7
  7.2 81.3 %all-gather.3.cloned.1.call-start = ((), (), s32[]{:S(2)}) async-start(), calls=%async_computation.10 | async-start | bytes 5242880 | tf_op jit(solution)/shard_map/all_gather | solution.py:122
  11.5 2.5 copy-start.9
  81.3 7.1 %copy-start.10 = (s32[128]{0:T(128)S(1)}, s32[128]{0:T(128)}, u32[]{:S(2)}) copy-start(s32[128]{0:T(128)} %param.14) | copy-start | bytes 1540
  81.3 37.0 %all-to-all-start.4 = ((bf16[128,3,2048]{2,1,0:T(4,128)(2,1)}), bf16[128,3,2048]{2,1,0:T(4,128)(2,1)}, u32[]{:S(2)}, u32[]{:S(2)}) async-start(bf16[128,3,2048]{2,1,0:T(4,128)(2,1)} %get-tuple-element.58), calls=%async_computation.4 | async-start | bytes 4194304 | tf_op jit(solution)/shard_map/all_to_all | solution.py:61
  118.2 130.2 %all-to-all-start.1 = ((bf16[32,64,2048]{2,1,0:T(8,128)(2,1)}), bf16[32,64,2048]{2,1,0:T(8,128)(2,1)}, u32[]{:S(2)}, u32[]{:S(2)}) async-start(bf16[32,64,2048]{2,1,0:T(8,128)(2,1)} %broadcast_select_fusion), calls=%async_computation.1 | async-start | bytes 16777216 | tf_op jit(solution)/shard_map/all_to_all | solution.py:128
  123.2 109.0 %all-gather.5.cloned.1.call-start = ((), (), s32[]{:S(2)}) async-start(), calls=%async_computation.11 | async-start | bytes 2621440 | tf_op jit(solution)/shard_map/all_gather | solution.py:123
  248.4 67.5 %all-to-all-start.2 = ((bf16[32,32,2048]{2,1,0:T(8,128)(2,1)}), bf16[32,32,2048]{2,1,0:T(8,128)(2,1)}, u32[]{:S(2)}, u32[]{:S(2)}) async-start(bf16[32,32,2048]{2,1,0:T(8,128)(2,1)} %broadcast_select_fusion.1), calls=%async_computation.2 | async-start | bytes 8388608 | tf_op jit(solution)/shard_map/all_to_all | solution.py:129
  264.2 5.2 copy-start.5
  315.9 7.2 %copy-start.6 = (bf16[384,2048]{1,0:T(8,128)(2,1)S(1)}, bf16[384,2048]{1,0:T(8,128)(2,1)}, u32[]{:S(2)}) copy-start(bf16[384,2048]{1,0:T(8,128)(2,1)} %reshape.242) | copy-start | bytes 4718596
  323.0 4.4 copy-start.11
  327.4 61.9 %all-to-all-start.7 = ((bf16[32,32,2048]{2,1,0:T(8,128)(2,1)}), bf16[32,32,2048]{2,1,0:T(8,128)(2,1)}, u32[]{:S(2)}, u32[]{:S(2)}) async-start(bf16[32,32,2048]{2,1,0:T(8,128)(2,1)} %bitcast.54), calls=%async_computation.8 | async-start | bytes 8388608 | tf_op jit(solution)/shard_map/all_to_all | solution.py:162
  389.3 130.7 %all-to-all-start.6 = ((bf16[32,64,2048]{2,1,0:T(8,128)(2,1)}), bf16[32,64,2048]{2,1,0:T(8,128)(2,1)}, u32[]{:S(2)}, u32[]{:S(2)}) async-start(bf16[32,64,2048]{2,1,0:T(8,128)(2,1)} %bitcast.53), calls=%async_computation.6 | async-start | bytes 16777216 | tf_op jit(solution)/shard_map/all_to_all | solution.py:155
  398.7 263.0 %reduce-scatter.5.cloned.1.call-start = ((), (), s32[]{:S(2)}) async-start(), calls=%async_computation.13 | async-start | bytes 2621440 | tf_op jit(solution)/shard_map/reduce_scatter | solution.py:177
  408.0 258.0 %reduce-scatter.3.cloned.1.call-start = ((), (), s32[]{:S(2)}) async-start(), calls=%async_computation.12 | async-start | bytes 5242880 | tf_op jit(solution)/shard_map/reduce_scatter | solution.py:174
  546.7 57.5 %all-to-all-start.5 = ((bf16[128,3,2048]{2,1,0:T(4,128)(2,1)}), bf16[128,3,2048]{2,1,0:T(4,128)(2,1)S(1)}, u32[]{:S(2)}, u32[]{:S(2)}) async-start(bf16[128,3,2048]{2,1,0:T(4,128)(2,1)} %reshape.243), calls=%async_computation.5 | async-start | bytes 4194304 | tf_op jit(solution)/shard_map/all_to_all | solution.py:69
  604.2 1.3 copy-start.3
  605.5 40.0 %all-to-all-start.3 = ((bf16[128,3,2048]{2,1,0:T(4,128)(2,1)}), bf16[128,3,2048]{2,1,0:T(4,128)(2,1)}, u32[]{:S(2)}, u32[]{:S(2)}) async-start(bf16[128,3,2048]{2,1,0:T(4,128)(2,1)} %reshape.240), calls=%async_computation.3 | async-start | bytes 4194304 | tf_op jit(solution)/shard_map/all_to_all | solution.py:68
  651.8 2.7 copy-start.2
  661.7 4.4 copy-start.4
  666.1 6.5 copy-start.1
Sparse Core Ops, SparseCore 0:
  10.3 72.6 all-gather.2
  126.3 105.8 all-gather.4
  408.2 106.6 reduce-scatter.4
  537.0 107.0 reduce-scatter.2
where the time goes:
time: 689 us; the launch traced here: 680 us
  waiting for transfers between devices  363 us (53%)
  starting transfers between devices  84.4 us (12%)
  local copies, waits for them, and re-layouts  71.7 us (10%)
  matrix products  60.3 us (9%)
  blocking collectives  44.3 us (6%)
  other arithmetic  41.2 us (6%)
  between operations  14.5 us (2%)
    all_gather x1, waiting for transfers between devices, on_device(): lax.all_gather(low_out, 'grp', axis=0, tiled=True)  107 us
    all_to_all x1, waiting for transfers between devices, on_device(): lax.all_to_all(grad_up.reshape(members, D // members, 2 * FF), 'dev', spl...  103 us
    all_to_all x1, waiting for transfers between devices, on_device(): lax.all_to_all(grad_down.reshape(members, FF // members, D), 'dev', split...  45 us
    all_to_all x1, blocking collectives, to_slots(): lax.all_to_all(payload_x, ('grp', 'dev'), split_axis=0, concat_axis=0, ti...  44.3 us
    all_to_all x1, waiting for transfers between devices, on_device(): lax.all_to_all(send_down, 'dev', split_axis=0, concat_axis=0, tiled=True)  38 us
    all_to_all x1, waiting for transfers between devices, to_sources(): lax.all_to_all(payload_out, ('grp', 'dev'), split_axis=0, concat_axis=0,...  25.2 us
    all_to_all x1, starting transfers between devices, to_sources(): lax.all_to_all(payload_dx, ('grp', 'dev'), split_axis=0, concat_axis=0, t...  24.6 us
    all_to_all x1, waiting for transfers between devices, to_sources(): lax.all_to_all(payload_dx, ('grp', 'dev'), split_axis=0, concat_axis=0, t...  22.4 us
  transfers between devices with their start and end apart: 11, of which 8 were waited for; matrix products, arithmetic and copies ran while one was open for 22% of the time, Pallas kernels for 0%

commit v1 on v0

--- a/solution.py
+++ b/solution.py
@@ -118,9 +118,22 @@
     group_expert = lax.dynamic_slice_in_dim(slot_expert, my_group * members, members)
     low_in = proj_in.astype(jnp.bfloat16)
     low_out = proj_out.astype(jnp.bfloat16)
+
+    def cubes_start(local_array, net_axis):
+        left_arr = jnp.concatenate(
+            lax.all_to_all(
+                jnp.stack([local_array] * lax.axis_size(net_axis)),
+                axis_name=net_axis,
+                split_axis=0,
+                concat_axis=0,
+            ),
+            axis=0,
+        )
+        return left_arr
+
     all_up, all_down = (
         lax.all_gather(low_in, "grp", axis=0, tiled=True),
-        lax.all_gather(low_out, "grp", axis=0, tiled=True),
+        cubes_start(low_out, "grp"),
     )
     send_up = jnp.take(all_up, group_expert, axis=0)
     send_down = jnp.take(all_down, group_expert, axis=0)

time: 689 us -> 709 us (1.029)
  waiting for transfers between devices: 363 us -> 387 us
    all_to_all x1, waiting for transfers between devices: 7.26 us -> 120 us  [on_device(): lax.all_to_all(send_up, 'dev', split_axis=0, concat_axis=0, tiled=True)]
    all_gather x1 -> x0, waiting for transfers between devices: 107 us -> none  [on_device(): lax.all_gather(low_out, 'grp', axis=0, tiled=True)]
    all_to_all x1, waiting for transfers between devices: 15.1 us -> 28.9 us  [to_slots(): lax.all_to_all(payload_dy, ('grp', 'dev'), split_axis=0, concat_axis=0, t...]
    all_to_all x0 -> x1, waiting for transfers between devices: none -> 10 us  [cubes_start(): lax.all_to_all(jnp.stack([local_array] * lax.axis_size(net_axis)), axis_n...]
    all_to_all x1, starting transfers between devices: 24.6 us -> 15.4 us  [to_sources(): lax.all_to_all(payload_dx, ('grp', 'dev'), split_axis=0, concat_axis=0, t...]
where the time goes in v1:
time: 709 us; the launch traced here: 699 us
  waiting for transfers between devices  387 us (55%)
  starting transfers between devices  80.5 us (11%)
  local copies, waits for them, and re-layouts  72.1 us (10%)
  matrix products  60.3 us (9%)
  blocking collectives  44.4 us (6%)
  other arithmetic  40.4 us (6%)
  between operations  14.5 us (2%)
    all_to_all x1, waiting for transfers between devices, on_device(): lax.all_to_all(send_up, 'dev', split_axis=0, concat_axis=0, tiled=True)  120 us
    all_to_all x1, waiting for transfers between devices, on_device(): lax.all_to_all(grad_up.reshape(members, D // members, 2 * FF), 'dev', spl...  99 us
    all_to_all x1, waiting for transfers between devices, on_device(): lax.all_to_all(grad_down.reshape(members, FF // members, D), 'dev', split...  45.8 us
    all_to_all x1, blocking collectives, to_slots(): lax.all_to_all(payload_x, ('grp', 'dev'), split_axis=0, concat_axis=0, ti...  44.4 us
    all_to_all x1, waiting for transfers between devices, on_device(): lax.all_to_all(send_down, 'dev', split_axis=0, concat_axis=0, tiled=True)  36.2 us
    all_to_all x1, waiting for transfers between devices, to_slots(): lax.all_to_all(payload_dy, ('grp', 'dev'), split_axis=0, concat_axis=0, t...  28.9 us
    all_to_all x1, waiting for transfers between devices, to_sources(): lax.all_to_all(payload_out, ('grp', 'dev'), split_axis=0, concat_axis=0,...  25.2 us
    all_to_all x1, waiting for transfers between devices, to_sources(): lax.all_to_all(payload_dx, ('grp', 'dev'), split_axis=0, concat_axis=0, t...  22.4 us
  transfers between devices with their start and end apart: 11, of which 8 were waited for; matrix products, arithmetic and copies ran while one was open for 22% of the time, Pallas kernels for 0%

profile of v1, /device:TPU:1, one launch (start us, length us, event | category | flops | bytes accessed | tf_op | source)
XLA Modules:
  0.0 699.4 jit_solution(12335312577771703270)
XLA Ops:
  7.3 2.8 convert_element_type.80
  11.9 2.4 convert_element_type.87
  16.8 3.1 gather_fusion.4
  19.9 4.0 gather.35
  24.3 3.1 gather_fusion
  27.5 5.2 gather.29
  32.6 4.3 broadcast_select_fusion.2
  36.9 44.4 %all_to_all.45 = bf16[128,3,2048]{2,1,0:T(4,128)(2,1)} all-to-all(bf16[128,3,2048]{2,1,0:T(4,128)(2,1)S(1)} %get-tuple-element.59), channel_id=1, replica_groups=mesh['grp'=4,'dev'=32] {'grp','dev'}, dimensions={0} | all-to-all | bytes 3145728 | tf_op jit(solution)/shard_map/all_to_all | solution.py:60
  81.4 6.6 all-to-all-start.5
  89.3 28.9 %all-to-all-done.5 = bf16[128,3,2048]{2,1,0:T(4,128)(2,1)S(1)} async-done(((bf16[128,3,2048]{2,1,0:T(4,128)(2,1)}), bf16[128,3,2048]{2,1,0:T(4,128)(2,1)S(1)}, u32[]{:S(2)}, u32[]{:S(2)}) %all-to-all-start.5) | async-done | bytes 1572896 | tf_op jit(solution)/shard_map/all_to_all | solution.py:61
  120.2 4.1 all-to-all-start.2
  124.4 7.2 %gather_fusion.1 = bf16[32,64,2048]{2,1,0:T(8,128)(2,1)} fusion(bf16[16,64,2048]{2,1,0:T(8,128)(2,1)} %all-gather.2.cloned.1.call-done, s32[1024]{0:T(1024)S(1)} %pad_clamp_fusion.2), kind=kCustom, calls=%fused_computation.1 | custom fusion | bytes 16777344 | tf_op jit(solution)/shard_map/jit(_take)/gather | solution.py:138
  131.6 7.5 %broadcast_select_fusion = bf16[32,64,2048]{2,1,0:T(8,128)(2,1)} fusion(bf16[32,64,2048]{2,1,0:T(8,128)(2,1)} %gather_fusion.1, pred[32]{0:T(512)(128)(4,1)S(1)} %get-tuple-element.53), kind=kLoop, calls=%fused_computation.8 | loop fusion | flops 4194304 | bytes 16777248 | tf_op jit(solution)/shard_map/jit(_take)/select_n | solution.py:138
  139.1 10.0 %all-to-all-done.2 = bf16[4,4,32,2048]{3,2,1,0:T(8,128)(2,1)S(1)} async-done(((bf16[4,4,32,2048]{3,2,1,0:T(8,128)(2,1)}), bf16[4,4,32,2048]{3,2,1,0:T(8,128)(2,1)S(1)}, u32[]{:S(2)}, u32[]{:S(2)}) %all-to-all-start.2) | async-done | bytes 2097184 | tf_op jit(solution)/shard_map/all_to_all | solution.py:124
  149.2 5.0 all-to-all-start.1
  154.1 2.8 gather_fusion.2
  156.9 4.6 broadcast_select_fusion.1
  161.5 119.5 %all-to-all-done.1 = bf16[32,64,2048]{2,1,0:T(8,128)(2,1)} async-done(((bf16[32,64,2048]{2,1,0:T(8,128)(2,1)}), bf16[32,64,2048]{2,1,0:T(8,128)(2,1)}, u32[]{:S(2)}, u32[]{:S(2)}) %all-to-all-start.1) | async-done | bytes 8388640 | tf_op jit(solution)/shard_map/all_to_all | solution.py:141
  281.0 15.1 %all-to-all-start.3 = ((bf16[32,32,2048]{2,1,0:T(8,128)(2,1)}), bf16[32,32,2048]{2,1,0:T(8,128)(2,1)}, u32[]{:S(2)}, u32[]{:S(2)}) async-start(bf16[32,32,2048]{2,1,0:T(8,128)(2,1)} %broadcast_select_fusion.1), calls=%async_computation.3 | async-start | bytes 8388608 | tf_op jit(solution)/shard_map/all_to_all | solution.py:142
  296.2 2.5 reshape.242
  298.7 5.2 reshape.248
  303.9 8.5 %fusion.40 = f32[384,2048]{1,0:T(8,128)} fusion(bf16[384,2048]{1,0:T(8,128)(2,1)S(1)} %copy-done.7, bf16[2048,2048]{1,0:T(8,128)(2,1)} %bitcast.4), kind=kOutput, calls=%fused_computation.89 | convolution fusion | flops 3221225472 | bytes 13107200 | tf_op jit(solution)/shard_map/dot_general | solution.py:24
  312.3 36.2 %all-to-all-done.3 = bf16[32,32,2048]{2,1,0:T(8,128)(2,1)} async-done(((bf16[32,32,2048]{2,1,0:T(8,128)(2,1)}), bf16[32,32,2048]{2,1,0:T(8,128)(2,1)}, u32[]{:S(2)}, u32[]{:S(2)}) %all-to-all-start.3) | async-done | bytes 4194336 | tf_op jit(solution)/shard_map/all_to_all | solution.py:142
  348.6 7.2 %multiply_convert_fusion.2 = (bf16[384,1024]{1,0:T(8,128)(2,1)}, bf16[384,1024]{1,0:T(8,128)(2,1)}, bf16[384,1024]{1,0:T(8,128)(2,1)S(1)}) fusion(f32[384,2048]{1,0:T(8,128)} %fusion.40, bf16[384,2048]{1,0:T(8,128)(2,1)} %reshape.248, bf16[1024,2048]{1,0:T(8,128)(2,1)} %bitcast.6), kind=kOutput, calls=%fused_computation.30 | convolution fusion | flops 1616510976 | bytes 11272192 | tf_op jit(solution)/shard_map/dot_general | solution.py:30
  355.8 4.3 convolution_convert_fusion.1
  360.1 9.7 %all-to-all-start.8 = ((bf16[32,32,2048]{2,1,0:T(8,128)(2,1)}), bf16[32,32,2048]{2,1,0:T(8,128)(2,1)}, u32[]{:S(2)}, u32[]{:S(2)}) async-start(bf16[32,32,2048]{2,1,0:T(8,128)(2,1)} %bitcast.56), calls=%async_computation.9 | async-start | bytes 8388608 | tf_op jit(solution)/shard_map/all_to_all | solution.py:175
  369.8 8.1 %convolution_convert_fusion = bf16[2048,2048]{1,0:T(8,128)(2,1)} fusion(bf16[384,2048]{1,0:T(8,128)(2,1)S(1)} %copy-done.7, bf16[384,1024]{1,0:T(8,128)(2,1)} %get-tuple-element.56, bf16[384,1024]{1,0:T(8,128)(2,1)} %get-tuple-element.55), kind=kOutput, calls=%fused_computation.9 | convolution fusion | flops 3228565504 | bytes 11534336 | tf_op jit(solution)/shard_map/dot_general | solution.py:39
  377.9 45.8 %all-to-all-done.8 = bf16[32,32,2048]{2,1,0:T(8,128)(2,1)} async-done(((bf16[32,32,2048]{2,1,0:T(8,128)(2,1)}), bf16[32,32,2048]{2,1,0:T(8,128)(2,1)}, u32[]{:S(2)}, u32[]{:S(2)}) %all-to-all-start.8) | async-done | bytes 4194336 | tf_op jit(solution)/shard_map/all_to_all | solution.py:175
  423.8 8.2 %all-to-all-start.7 = ((bf16[32,64,2048]{2,1,0:T(8,128)(2,1)}), bf16[32,64,2048]{2,1,0:T(8,128)(2,1)}, u32[]{:S(2)}, u32[]{:S(2)}) async-start(bf16[32,64,2048]{2,1,0:T(8,128)(2,1)} %bitcast.55), calls=%async_computation.7 | async-start | bytes 16777216 | tf_op jit(solution)/shard_map/all_to_all | solution.py:168
  432.0 6.8 fusion.7
  438.8 2.5 copy.90
  441.3 8.8 %reduce-scatter.3.cloned.1.call-start = ((), (), s32[]{:S(2)}) async-start(), calls=%async_computation.12 | async-start | bytes 5242880 | tf_op jit(solution)/shard_map/reduce_scatter | solution.py:187
  450.1 99.0 %all-to-all-done.7 = bf16[32,64,2048]{2,1,0:T(8,128)(2,1)} async-done(((bf16[32,64,2048]{2,1,0:T(8,128)(2,1)}), bf16[32,64,2048]{2,1,0:T(8,128)(2,1)}, u32[]{:S(2)}, u32[]{:S(2)}) %all-to-all-start.7) | async-done | bytes 8388640 | tf_op jit(solution)/shard_map/all_to_all | solution.py:168
  549.1 12.5 %fusion.4 = bf16[16,64,2048]{2,0,1:T(8,128)(2,1)S(1)} fusion(bf16[32,64,2048]{2,1,0:T(8,128)(2,1)} %all-to-all-done.7, s32[32]{0:T(128)S(1)} %get-tuple-element.54), kind=kOutput, calls=%fused_computation.14 | convolution fusion | flops 136315392 | bytes 12583040 | tf_op jit(solution)/shard_map/ed,drc->erc/dot_general | solution.py:184
  561.6 4.3 copy.88
  565.9 7.5 %convolution_convert_fusion.2 = bf16[384,2048]{1,0:T(8,128)(2,1)S(1)} fusion(bf16[2048,2048]{1,0:T(8,128)(2,1)} %bitcast.4, bf16[384,1024]{1,0:T(8,128)(2,1)} %get-tuple-element.56, bf16[384,1024]{1,0:T(8,128)(2,1)} %get-tuple-element.55), kind=kOutput, calls=%fused_computation.17 | convolution fusion | flops 3225157632 | bytes 11534336 | tf_op jit(solution)/shard_map/dot_general | solution.py:36
  575.7 15.4 %all-to-all-start.6 = ((bf16[128,3,2048]{2,1,0:T(4,128)(2,1)}), bf16[128,3,2048]{2,1,0:T(4,128)(2,1)S(1)}, u32[]{:S(2)}, u32[]{:S(2)}) async-start(bf16[128,3,2048]{2,1,0:T(4,128)(2,1)} %reshape.249), calls=%async_computation.6 | async-start | bytes 4194304 | tf_op jit(solution)/shard_map/all_to_all | solution.py:69
  591.1 5.4 convolution_convert_fusion.3
  596.5 5.2 reshape.246
  601.7 22.4 %all-to-all-done.6 = bf16[128,3,2048]{2,1,0:T(4,128)(2,1)S(1)} async-done(((bf16[128,3,2048]{2,1,0:T(4,128)(2,1)}), bf16[128,3,2048]{2,1,0:T(4,128)(2,1)S(1)}, u32[]{:S(2)}, u32[]{:S(2)}) %all-to-all-start.6) | async-done | bytes 1572896 | tf_op jit(solution)/shard_map/all_to_all | solution.py:69
  625.4 7.5 %all-to-all-start.4 = ((bf16[128,3,2048]{2,1,0:T(4,128)(2,1)}), bf16[128,3,2048]{2,1,0:T(4,128)(2,1)}, u32[]{:S(2)}, u32[]{:S(2)}) async-start(bf16[128,3,2048]{2,1,0:T(4,128)(2,1)} %reshape.246), calls=%async_computation.4 | async-start | bytes 4194304 | tf_op jit(solution)/shard_map/all_to_all | solution.py:68
  633.5 3.9 reshape.250
  640.3 25.2 %all-to-all-done.4 = bf16[128,3,2048]{2,1,0:T(4,128)(2,1)} async-done(((bf16[128,3,2048]{2,1,0:T(4,128)(2,1)}), bf16[128,3,2048]{2,1,0:T(4,128)(2,1)}, u32[]{:S(2)}, u32[]{:S(2)}) %all-to-all-start.4) | async-done | bytes 1572896 | tf_op jit(solution)/shard_map/all_to_all | solution.py:68
  665.4 3.9 reshape.247
  671.7 2.7 gather.33
  676.8 2.9 copy_select_fusion
  681.6 4.4 multiply_subtract_fusion.1
  685.9 6.5 multiply_subtract_fusion
  (81 shorter events, 21.8 us)
Async XLA Ops:
  7.2 17.2 %copy-start = (bf16[128,2048]{1,0:T(8,128)(2,1)S(1)}, bf16[128,2048]{1,0:T(8,128)(2,1)}, u32[]{:S(2)}) copy-start(bf16[128,2048]{1,0:T(8,128)(2,1)} %param.11) | copy-start | bytes 1572868
  7.2 2.9 copy-start.10
  7.2 3.6 copy-start.9
  7.2 117.2 %all-gather.2.cloned.1.call-start = ((), (), s32[]{:S(2)}) async-start(), calls=%async_computation.11 | async-start | bytes 5242880 | tf_op jit(solution)/shard_map/all_gather | solution.py:135
  11.9 2.5 copy-start.11
  81.4 36.8 %all-to-all-start.5 = ((bf16[128,3,2048]{2,1,0:T(4,128)(2,1)}), bf16[128,3,2048]{2,1,0:T(4,128)(2,1)S(1)}, u32[]{:S(2)}, u32[]{:S(2)}) async-start(bf16[128,3,2048]{2,1,0:T(4,128)(2,1)} %get-tuple-element.58), calls=%async_computation.5 | async-start | bytes 4194304 | tf_op jit(solution)/shard_map/all_to_all | solution.py:61
  118.2 2.0 copy-start.4
  120.0 4.3 copy-start.12
  120.2 28.9 %all-to-all-start.2 = ((bf16[4,4,32,2048]{3,2,1,0:T(8,128)(2,1)}), bf16[4,4,32,2048]{3,2,1,0:T(8,128)(2,1)S(1)}, u32[]{:S(2)}, u32[]{:S(2)}) async-start(bf16[4,4,32,2048]{3,2,1,0:T(8,128)(2,1)} %stack.2), calls=%async_computation.2 | async-start | bytes 4194304 | tf_op jit(solution)/shard_map/all_to_all | solution.py:124
  149.2 131.9 %all-to-all-start.1 = ((bf16[32,64,2048]{2,1,0:T(8,128)(2,1)}), bf16[32,64,2048]{2,1,0:T(8,128)(2,1)}, u32[]{:S(2)}, u32[]{:S(2)}) async-start(bf16[32,64,2048]{2,1,0:T(8,128)(2,1)} %broadcast_select_fusion), calls=%async_computation.1 | async-start | bytes 16777216 | tf_op jit(solution)/shard_map/all_to_all | solution.py:141
  161.5 134.7 %copy-start.3 = (bf16[128,3,2048]{2,1,0:T(4,128)(2,1)S(1)}, bf16[128,3,2048]{2,1,0:T(4,128)(2,1)}, u32[]{:S(2)}) copy-start(bf16[128,3,2048]{2,1,0:T(4,128)(2,1)} %all_to_all.45) | copy-start | bytes 4718596
  281.0 67.6 %all-to-all-start.3 = ((bf16[32,32,2048]{2,1,0:T(8,128)(2,1)}), bf16[32,32,2048]{2,1,0:T(8,128)(2,1)}, u32[]{:S(2)}, u32[]{:S(2)}) async-start(bf16[32,32,2048]{2,1,0:T(8,128)(2,1)} %broadcast_select_fusion.1), calls=%async_computation.3 | async-start | bytes 8388608 | tf_op jit(solution)/shard_map/all_to_all | solution.py:142
  298.7 5.2 copy-start.7
  348.6 7.2 %copy-start.8 = (bf16[384,2048]{1,0:T(8,128)(2,1)S(1)}, bf16[384,2048]{1,0:T(8,128)(2,1)}, u32[]{:S(2)}) copy-start(bf16[384,2048]{1,0:T(8,128)(2,1)} %reshape.248) | copy-start | bytes 4718596
  355.8 4.4 copy-start.13
  360.1 63.7 %all-to-all-start.8 = ((bf16[32,32,2048]{2,1,0:T(8,128)(2,1)}), bf16[32,32,2048]{2,1,0:T(8,128)(2,1)}, u32[]{:S(2)}, u32[]{:S(2)}) async-start(bf16[32,32,2048]{2,1,0:T(8,128)(2,1)} %bitcast.56), calls=%async_computation.9 | async-start | bytes 8388608 | tf_op jit(solution)/shard_map/all_to_all | solution.py:175
  423.8 125.3 %all-to-all-start.7 = ((bf16[32,64,2048]{2,1,0:T(8,128)(2,1)}), bf16[32,64,2048]{2,1,0:T(8,128)(2,1)}, u32[]{:S(2)}, u32[]{:S(2)}) async-start(bf16[32,64,2048]{2,1,0:T(8,128)(2,1)} %bitcast.55), calls=%async_computation.7 | async-start | bytes 16777216 | tf_op jit(solution)/shard_map/all_to_all | solution.py:168
  431.9 249.6 %reduce-scatter.5.cloned.1.call-start = ((), (), s32[]{:S(2)}) async-start(), calls=%async_computation.13 | async-start | bytes 2621440 | tf_op jit(solution)/shard_map/reduce_scatter | solution.py:190
  441.3 244.6 %reduce-scatter.3.cloned.1.call-start = ((), (), s32[]{:S(2)}) async-start(), calls=%async_computation.12 | async-start | bytes 5242880 | tf_op jit(solution)/shard_map/reduce_scatter | solution.py:187
  575.7 48.4 %all-to-all-start.6 = ((bf16[128,3,2048]{2,1,0:T(4,128)(2,1)}), bf16[128,3,2048]{2,1,0:T(4,128)(2,1)S(1)}, u32[]{:S(2)}, u32[]{:S(2)}) async-start(bf16[128,3,2048]{2,1,0:T(4,128)(2,1)} %reshape.249), calls=%async_computation.6 | async-start | bytes 4194304 | tf_op jit(solution)/shard_map/all_to_all | solution.py:69
  624.1 1.3 copy-start.5
  625.4 40.0 %all-to-all-start.4 = ((bf16[128,3,2048]{2,1,0:T(4,128)(2,1)}), bf16[128,3,2048]{2,1,0:T(4,128)(2,1)}, u32[]{:S(2)}, u32[]{:S(2)}) async-start(bf16[128,3,2048]{2,1,0:T(4,128)(2,1)} %reshape.246), calls=%async_computation.4 | async-start | bytes 4194304 | tf_op jit(solution)/shard_map/all_to_all | solution.py:68
  671.7 2.7 copy-start.2
  681.6 4.4 copy-start.6
  685.9 6.5 copy-start.1
Sparse Core Ops, SparseCore 0:
  10.3 72.6 all-gather.1
  441.4 95.6 reduce-scatter.4
  566.0 97.9 reduce-scatter.2
